TPU v7x, 32 devices: a whole 2x2x4 slice. The times are simulated.
32 devices in a mesh: cfg: 2 (over core), seq: 4 (over z), blk: 4 (over y, x).
Axes of the slice: x: 2, y: 2, z: 4, core: 2. Of those that a mesh axis runs over, the one named last changes fastest.
Arguments:
- img_hidden: bfloat16 [2, 2, 2048, 1536], P('cfg', None, 'seq', 'blk'), may hold values from -15 to 15
- txt_hidden: bfloat16 [2, 2, 160, 1536], P('cfg', None, 'seq', 'blk'), may hold values from -6 to 6
- img_mod: float32 [2, 2, 6, 1536], P('cfg'), may hold values from -9 to 9
- txt_mod: float32 [2, 2, 2, 1536], P('cfg'), may hold values from -3 to 3
- out_mod: float32 [2, 2, 2, 1536], P('cfg'), may hold values from -3 to 3
- w_qkv: bfloat16 [3, 1536, 1536], P(None, None, 'blk'), may hold values from -0.25 to 0.25
- w_txt_kv: bfloat16 [2, 1536, 1536], P(None, None, 'blk'), may hold values from -0.25 to 0.25
- w_out: bfloat16 [1536, 1536], P('blk'), may hold values from -0.15625 to 0.15625
- w_fc1: bfloat16 [1536, 6144], P(None, 'blk'), may hold values from -0.15625 to 0.15625
- w_fc2: bfloat16 [6144, 1536], P('blk'), may hold values from -0.078125 to 0.078125
- w_proj: bfloat16 [1536, 64], P('blk'), may hold values from -0.15625 to 0.15625
- latent: float32 [2, 2048, 64], P(None, 'seq', 'cfg'), may hold values from -6 to 6
- lengths: int32 [2, 2], P('cfg'), may hold values from 1 to 154, as said below
- t_index: int32 [2], replicated, may hold values from 0 to 24
- stride: int32 [2], replicated, may hold values from 1 to 4
- guide: float32 [2], replicated, may hold values from 4 to 8
Outputs:
- new_latent: float32 [2, 2048, 64], P(None, 'seq', 'cfg')
- update_max: float32 [2], replicated
Inputs may be any that keep to these rules, and one draw needn't show every extreme that they name: `lengths`: at least one entry equals 154.
All inputs are finite; a program needn't handle non-finite values.
Results may differ from a plain program's by a relative error of at most 0.015.
Values may be sent and summed in bfloat16 or wider, within the bound.
A program may use at most 192 MiB of HBM per device.

v0:
```python
import jax
import jax.numpy as jnp
from jax import lax
from jax.sharding import PartitionSpec as P

HEAD = 64
STEPS = 28
EPSILON = 1e-06
BLOCK_ROWS = 512


def from_partner(value, axis, bit):
    return lax.ppermute(value, axis, [(i, i ^ 1 << bit) for i in range(lax.axis_size(axis))])


def normalize(values):
    values = values.astype(jnp.float32)
    center = jnp.mean(values, axis=-1, keepdims=True)
    spread = jnp.mean(jnp.square(values - center), axis=-1, keepdims=True)
    return (values - center) * lax.rsqrt(spread + EPSILON)


def modulate(values, scale_row, shift_row):
    return (normalize(values) * (1.0 + scale_row[:, None, :]) + shift_row[:, None, :]).astype(
        jnp.bfloat16
    )


def project(values, weight):
    flat_rows = values.reshape(-1, values.shape[-1])
    result = jnp.dot(flat_rows, weight, preferred_element_type=jnp.float32)
    return result.reshape(values.shape[:-1] + (weight.shape[-1],))


def noise_level(step_index):
    remain = 1.0 - step_index.astype(jnp.float32) / STEPS
    return 3.0 * remain / (1.0 + 2.0 * remain)


def own_columns(values, column_block, shard_width):
    return lax.dynamic_slice_in_dim(
        values, column_block * shard_width, shard_width, values.ndim - 1
    )


def per_device(
    img_hidden,
    txt_hidden,
    img_mod,
    txt_mod,
    out_mod,
    w_qkv,
    w_txt_kv,
    w_out,
    w_fc1,
    w_fc2,
    w_proj,
    latent,
    lengths,
    t_index,
    stride,
    guide,
):
    column_block = lax.axis_index("blk")
    shard_width = img_hidden.shape[3]
    model_width = shard_width * lax.axis_size("blk")
    image_full, text_full = (
        lax.all_gather(img_hidden[0], "blk", axis=2, tiled=True),
        lax.all_gather(txt_hidden[0], "blk", axis=2, tiled=True),
    )
    image_mod = img_mod[0]
    prompts = image_full.shape[0]
    img_rows = image_full.shape[1]
    attn_in = modulate(image_full, image_mod[:, 1], image_mod[:, 0])
    queries = project(attn_in, w_qkv[0]).astype(jnp.bfloat16)
    keys_img = project(attn_in, w_qkv[1]).astype(jnp.bfloat16)
    values_img = project(attn_in, w_qkv[2]).astype(jnp.bfloat16)
    text_norm = modulate(text_full, txt_mod[0][:, 0], txt_mod[0][:, 1])
    text_keys = project(text_norm, w_txt_kv[0]).astype(jnp.bfloat16)
    text_values = project(text_norm, w_txt_kv[1]).astype(jnp.bfloat16)
    head_width = queries.shape[2]
    head_count = head_width // HEAD
    query_heads = queries.reshape(prompts, img_rows, head_count, HEAD)
    text_limit = lengths[0]

    def attend_block(running_state, key_block, value_block, live_mask):
        accumulated, running, denominator = running_state
        key_count = key_block.shape[1]
        key_heads = key_block.reshape(prompts, key_count, head_count, HEAD)
        value_heads = value_block.reshape(prompts, key_count, head_count, HEAD)
        scores = jnp.einsum(
            "pqhe,pkhe->phqk", query_heads, key_heads, preferred_element_type=jnp.float32
        ) * HEAD ** (-0.5)
        if live_mask is not None:
            scores = jnp.where(live_mask[:, None, None, :], scores, -jnp.inf)
        updated = jnp.maximum(running, jnp.max(scores, axis=-1))
        factor = jnp.exp(running - updated)
        weights = jnp.exp(scores - updated[..., None])
        denominator = denominator * factor + jnp.sum(weights, axis=-1)
        mixed_values = jnp.einsum(
            "phqk,pkhe->phqe",
            weights.astype(jnp.bfloat16),
            value_heads,
            preferred_element_type=jnp.float32,
        )
        accumulated = accumulated * factor[..., None] + mixed_values
        return (accumulated, updated, denominator)

    initial = (
        jnp.zeros((prompts, head_count, img_rows, HEAD), jnp.float32),
        jnp.full((prompts, head_count, img_rows), -1e30, jnp.float32),
        jnp.zeros((prompts, head_count, img_rows), jnp.float32),
    )
    running_state = initial
    key_piece = lax.all_gather(keys_img, "seq", axis=1, tiled=True)
    value_piece = lax.all_gather(values_img, "seq", axis=1, tiled=True)
    key_count = key_piece.shape[1]
    blocks = key_count // BLOCK_ROWS
    key_split = key_piece.reshape(prompts, blocks, BLOCK_ROWS, head_width).transpose(1, 0, 2, 3)
    value_split = value_piece.reshape(prompts, blocks, BLOCK_ROWS, head_width).transpose(1, 0, 2, 3)

    def scan_step(state_now, operands):
        key_block, value_block = operands
        return (attend_block(state_now, key_block, value_block, None), None)

    running_state, unused = lax.scan(scan_step, running_state, (key_split, value_split))
    all_text_keys, all_text_values = (
        lax.all_gather(text_keys, "seq", axis=1, tiled=True),
        lax.all_gather(text_values, "seq", axis=1, tiled=True),
    )
    slot_index = jnp.arange(all_text_keys.shape[1], dtype=jnp.int32)
    text_mask = slot_index[None, :] < text_limit[:, None]
    accumulated, running, denominator = attend_block(
        running_state, all_text_keys, all_text_values, text_mask
    )
    attended = (accumulated / denominator[..., None]).astype(jnp.bfloat16)
    attended = attended.transpose(0, 2, 1, 3).reshape(prompts, img_rows, head_width)
    attn_part = project(attended, w_out)
    attn_sum = lax.psum(attn_part.astype(jnp.bfloat16), "blk").astype(jnp.float32)
    resid_full = (image_full.astype(jnp.float32) + image_mod[:, 2][:, None, :] * attn_sum).astype(
        jnp.bfloat16
    )
    resid_one = own_columns(resid_full, column_block, shard_width)
    mlp_in = modulate(resid_full, image_mod[:, 4], image_mod[:, 3])
    hidden_units = jax.nn.gelu(project(mlp_in, w_fc1), approximate=True).astype(jnp.bfloat16)
    mlp_sum = lax.psum_scatter(
        project(hidden_units, w_fc2).astype(jnp.bfloat16), "blk", scatter_dimension=2, tiled=True
    ).astype(jnp.float32)
    gate_mlp = own_columns(image_mod[:, 5], column_block, shard_width)
    resid_two = (resid_one.astype(jnp.float32) + gate_mlp[:, None, :] * mlp_sum).astype(
        jnp.bfloat16
    )
    stream = resid_two.astype(jnp.float32)
    row_sum, row_squares = lax.psum(
        (jnp.sum(stream, axis=-1), jnp.sum(stream * stream, axis=-1)), "blk"
    )
    center = row_sum / model_width
    spread = row_squares / model_width - center * center
    final_mod = out_mod[0]
    final_scale = own_columns(final_mod[:, 0], column_block, shard_width)
    final_shift = own_columns(final_mod[:, 1], column_block, shard_width)
    final_in = (
        (stream - center[..., None])
        * lax.rsqrt(spread[..., None] + EPSILON)
        * (1.0 + final_scale[:, None, :])
        + final_shift[:, None, :]
    ).astype(jnp.bfloat16)
    velocity_part = project(final_in, w_proj)
    half_index = lax.axis_index("cfg")
    channel_width = latent.shape[2]
    guide_scale = guide[:, None, None]
    velocity = lax.psum(velocity_part.astype(jnp.bfloat16), "blk").astype(jnp.float32)
    outgoing = own_columns(velocity, 1 - half_index, channel_width)
    other_half = from_partner(outgoing.astype(jnp.bfloat16), "cfg", 0).astype(outgoing.dtype)
    own_half = own_columns(velocity, half_index, channel_width)
    velocity_cond = jnp.where(half_index == 0, own_half, other_half)
    velocity_uncond = jnp.where(half_index == 0, other_half, own_half)
    guided = velocity_uncond + guide_scale * (velocity_cond - velocity_uncond)
    step_size = noise_level(t_index + stride) - noise_level(t_index)
    update = step_size[:, None, None] * guided
    new_latent = latent + update
    local_peak = jnp.max(jnp.abs(update), axis=(1, 2))
    peak_value = lax.pmax(local_peak, ("cfg", "seq"))
    return (new_latent, peak_value)


def solution(mesh):
    placed = (
        P("cfg", None, "seq", "blk"),
        P("cfg", None, "seq", "blk"),
        P("cfg", None, None, None),
        P("cfg", None, None, None),
        P("cfg", None, None, None),
        P(None, None, "blk"),
        P(None, None, "blk"),
        P("blk", None),
        P(None, "blk"),
        P("blk", None),
        P("blk", None),
        P(None, "seq", "cfg"),
        P("cfg", None),
        P(),
        P(),
        P(),
    )
    return jax.shard_map(
        per_device,
        mesh=mesh,
        in_specs=placed,
        out_specs=(P(None, "seq", "cfg"), P()),
        check_vma=False,
    )
```

profile of v0, /device:TPU:0, one launch (start us, length us, event | category | flops | bytes accessed | tf_op | source)
XLA Modules:
  0.0 552.0 jit_solution(2850391820597721948)
XLA Ops:
  9.6 46.8 %all-gather.10.cloned.1.call-done = bf16[1,2,512,1536]{3,2,1,0:T(8,128)(2,1)} async-done(((bf16[1,2,512,384]{3,2,1,0:T(8,128)(2,1)}), bf16[1,2,512,1536]{3,2,1,0:T(8,128)(2,1)}) %all-gather.10.cloned.1.call-update) | async-done | bytes 3145744 | tf_op jit(solution)/shard_map/all_gather | solution.py:68
  60.2 4.0 convolution_convert_fusion.1
  64.4 5.0 convolution_convert_fusion.3
  69.5 9.2 %all-gather.1 = bf16[1,2,40,1536]{3,2,1,0:T(8,128)(2,1)S(1)} all-gather(bf16[1,2,40,384]{3,2,1,0:T(8,128)(2,1)S(1)} %copy-done.12), channel_id=3, replica_groups=mesh['cfg'=2,'seq'=4,'blk'=4] {'blk'}, dimensions={3}, use_global_device_ids=true | all-gather | bytes 307200 | tf_op jit(solution)/shard_map/all_gather | solution.py:69
  80.8 16.4 %all_gather.22 = bf16[2,160,384]{2,1,0:T(8,128)(2,1)} all-gather(bf16[2,40,384]{2,1,0:T(8,128)(2,1)S(1)} %fusion.79), channel_id=1, replica_groups=mesh['cfg'=2,'seq'=4,'blk'=4] {'seq'}, dimensions={1}, use_global_device_ids=true | all-gather | bytes 307200 | tf_op jit(solution)/shard_map/all_gather | solution.py:128
  100.0 16.7 %all_gather.23 = bf16[2,160,384]{2,1,0:T(8,128)(2,1)S(1)} all-gather(bf16[2,40,384]{2,1,0:T(8,128)(2,1)S(1)} %fusion.82), channel_id=1, replica_groups=mesh['cfg'=2,'seq'=4,'blk'=4] {'seq'}, dimensions={1}, use_global_device_ids=true | all-gather | bytes 307200 | tf_op jit(solution)/shard_map/all_gather | solution.py:129
  117.6 4.0 convolution_convert_fusion.2
  122.5 3.4 fusion.41
  125.9 9.6 %all-gather.8.cloned.1.call-done = bf16[2,2048,384]{2,1,0:T(8,128)(2,1)} async-done(((bf16[2,512,384]{2,1,0:T(8,128)(2,1)}), bf16[2,2048,384]{2,1,0:T(8,128)(2,1)}) %all-gather.8.cloned.1.call-update) | async-done | bytes 3145744 | tf_op jit(solution)/shard_map/all_gather | solution.py:116
  135.5 4.7 copy.38
  140.2 59.2 %all-gather.6.cloned.1.call-done = bf16[2,2048,384]{2,1,0:T(8,128)(2,1)} async-done(((bf16[2,512,384]{2,1,0:T(8,128)(2,1)}), bf16[2,2048,384]{2,1,0:T(8,128)(2,1)}) %all-gather.6.cloned.1.call-update) | async-done | bytes 3145744 | tf_op jit(solution)/shard_map/all_gather | solution.py:115
  199.4 4.7 copy.36
  204.1 87.5 %while.15 = (s32[]{:T(128)}, f32[2,6,512,64]{2,3,1,0:T(8,128)S(1)}, f32[2,6,512]{2,1,0:T(8,128)}, f32[2,6,512]{2,1,0:T(8,128)}, bf16[4,2,512,384]{2,3,1,0:T(8,12...) while((s32[]{:T(128)}, f32[2,6,512,64]{2,3,1,0:T(8,128)S(1)}, ...), condition=%wide.region_5.0_spmd.clone, body=%wide.region_2.5_spmd.clone.sunk | while | flops 831682560 | bytes 97419496 | solution.py:126
  205.5 8.1 %bitcast_reduce_fusion.2 = (f32[2,6,512]{2,1,0:T(8,128)}, f32[2,6,512,512]{3,2,1,0:T(8,128)}) fusion(bf16[2,512,6,64]{1,3,2,0:T(8,128)(2,1)S(1)} %bitcast.165, bf16[2,512,6,64]{1,3,2,0:T(8,128)(2,1)} %get-tuple-element.199), kind=kOutput, calls=%fused_computation.1.clone.1 | convolution fusion | flops 408938496 | bytes 14180352 | tf_op jit(solution)/shard_map/while/body/eval_jaxpr/pqhe,pkhe->phqk/dot_general | solution.py:91
  214.4 6.8 %fusion.134 = f32[2,6,512]{2,1,0:T(8,128)S(1)} fusion(f32[2,6,512,512]{3,2,1,0:T(8,128)} %get-tuple-element.172, f32[2,6,512]{2,1,0:T(8,128)S(1)} %select_maximum_fusion.2), kind=kLoop, calls=%fused_computation.3.clone.1 | loop fusion | flops 9431040 | bytes 12632064 | tf_op jit(solution)/shard_map/while/body/eval_jaxpr/reduce_sum | solution.py:99
  227.4 8.1 %bitcast_reduce_fusion.2 = (f32[2,6,512]{2,1,0:T(8,128)}, f32[2,6,512,512]{3,2,1,0:T(8,128)}) fusion(bf16[2,512,6,64]{1,3,2,0:T(8,128)(2,1)S(1)} %bitcast.165, bf16[2,512,6,64]{1,3,2,0:T(8,128)(2,1)} %get-tuple-element.199), kind=kOutput, calls=%fused_computation.1.clone.1 | convolution fusion | flops 408938496 | bytes 14180352 | tf_op jit(solution)/shard_map/while/body/eval_jaxpr/pqhe,pkhe->phqk/dot_general | solution.py:91
  236.3 6.8 %fusion.134 = f32[2,6,512]{2,1,0:T(8,128)S(1)} fusion(f32[2,6,512,512]{3,2,1,0:T(8,128)} %get-tuple-element.172, f32[2,6,512]{2,1,0:T(8,128)S(1)} %select_maximum_fusion.2), kind=kLoop, calls=%fused_computation.3.clone.1 | loop fusion | flops 9431040 | bytes 12632064 | tf_op jit(solution)/shard_map/while/body/eval_jaxpr/reduce_sum | solution.py:99
  249.3 8.1 %bitcast_reduce_fusion.2 = (f32[2,6,512]{2,1,0:T(8,128)}, f32[2,6,512,512]{3,2,1,0:T(8,128)}) fusion(bf16[2,512,6,64]{1,3,2,0:T(8,128)(2,1)S(1)} %bitcast.165, bf16[2,512,6,64]{1,3,2,0:T(8,128)(2,1)} %get-tuple-element.199), kind=kOutput, calls=%fused_computation.1.clone.1 | convolution fusion | flops 408938496 | bytes 14180352 | tf_op jit(solution)/shard_map/while/body/eval_jaxpr/pqhe,pkhe->phqk/dot_general | solution.py:91
  258.2 6.8 %fusion.134 = f32[2,6,512]{2,1,0:T(8,128)S(1)} fusion(f32[2,6,512,512]{3,2,1,0:T(8,128)} %get-tuple-element.172, f32[2,6,512]{2,1,0:T(8,128)S(1)} %select_maximum_fusion.2), kind=kLoop, calls=%fused_computation.3.clone.1 | loop fusion | flops 9431040 | bytes 12632064 | tf_op jit(solution)/shard_map/while/body/eval_jaxpr/reduce_sum | solution.py:99
  271.2 8.1 %bitcast_reduce_fusion.2 = (f32[2,6,512]{2,1,0:T(8,128)}, f32[2,6,512,512]{3,2,1,0:T(8,128)}) fusion(bf16[2,512,6,64]{1,3,2,0:T(8,128)(2,1)S(1)} %bitcast.165, bf16[2,512,6,64]{1,3,2,0:T(8,128)(2,1)} %get-tuple-element.199), kind=kOutput, calls=%fused_computation.1.clone.1 | convolution fusion | flops 408938496 | bytes 14180352 | tf_op jit(solution)/shard_map/while/body/eval_jaxpr/pqhe,pkhe->phqk/dot_general | solution.py:91
  280.1 6.8 %fusion.134 = f32[2,6,512]{2,1,0:T(8,128)S(1)} fusion(f32[2,6,512,512]{3,2,1,0:T(8,128)} %get-tuple-element.172, f32[2,6,512]{2,1,0:T(8,128)S(1)} %select_maximum_fusion.2), kind=kLoop, calls=%fused_computation.3.clone.1 | loop fusion | flops 9431040 | bytes 12632064 | tf_op jit(solution)/shard_map/while/body/eval_jaxpr/reduce_sum | solution.py:99
  292.5 3.4 fusion.47
  298.1 3.5 convolution_convert_fusion
  301.8 85.9 %all-reduce.4.cloned.1.call-done = bf16[2,512,1536]{2,1,0:T(8,128)(2,1)} async-done(((bf16[2,512,1536]{2,1,0:T(8,128)(2,1)}), bf16[2,512,1536]{2,1,0:T(8,128)(2,1)}) %all-reduce.4.cloned.1.call-update) | async-done | bytes 3145744 | tf_op jit(solution)/shard_map/psum | solution.py:139
  387.7 4.0 convert_reduce_fusion.1
  394.4 15.8 %fusion.38 = bf16[2,512,1536]{2,1,0:T(8,128)(2,1)} fusion(bf16[1536,1536]{1,0:T(8,128)(2,1)} %param.27, bf16[1536,1536]{1,0:T(8,128)(2,1)} %param.26, bf16[2,512,1536]{2,1,0:T(8,128)(2,1)} %copy-done.4, f32[2,1536]{1,0:T(2,128)S(1)} %get-tuple-element.113, f32[2,1536]{1,0:T(2,128)S(1)} %get-tuple-element.114, f32[2,512]{1,0:T(2,128)S(1)} %add_rsqrt_fusion.1, ...), kind=kOutput, calls=%fused_computation.50 | convolution fusion | flops 9688842240 | bytes 15761408 | tf_op jit(solution)/shard_map/dot_general | solution.py:31
  410.2 8.7 %copy.44 = bf16[2,512,1536]{1,0,2:T(2,128)(2,1)} copy(bf16[2,512,1536]{2,1,0:T(8,128)(2,1)} %fusion.38) | data formatting | bytes 6291456
  418.9 4.4 copy.57
  424.2 43.3 %reduce-scatter.4.cloned.1.call-done = bf16[384,1024]{1,0:T(8,128)(2,1)} async-done(((bf16[1536,1024]{1,0:T(8,128)(2,1)}), bf16[384,1024]{1,0:T(8,128)(2,1)}) %reduce-scatter.4.cloned.1.call-update) | async-done | bytes 786448
  472.4 9.1 %all-reduce = (f32[2,512]{1,0:T(2,128)S(1)}, f32[2,512]{1,0:T(2,128)S(1)}) all-reduce(f32[2,512]{1,0:T(2,128)S(1)} %get-tuple-element.69, f32[2,512]{1,0:T(2,128)S(1)} %get-tuple-element.68), channel_id=1, replica_groups=mesh['cfg'=2,'seq'=4,'blk'=4] {'blk'}, use_global_device_ids=true, to_apply=%region_17.18 | all-reduce | flops 2048 | bytes 16384 | tf_op jit(solution)/shard_map/psum | solution.py:154
  482.7 42.1 %all-reduce.6.cloned.1.call-done = bf16[2,512,64]{1,2,0:T(8,128)(2,1)} async-done(((bf16[2,512,64]{1,2,0:T(8,128)(2,1)}), bf16[2,512,64]{1,2,0:T(8,128)(2,1)}) %all-reduce.6.cloned.1.call-update) | async-done | bytes 131088 | tf_op jit(solution)/shard_map/psum | solution.py:172
  527.9 17.2 %pmax.7 = f32[2]{0:T(128)} all-reduce(f32[2]{0:T(128)S(1)} %get-tuple-element.97), channel_id=1, replica_groups=mesh['cfg'=2,'seq'=4,'blk'=4] {'cfg','seq'}, use_global_device_ids=true, to_apply=%region_20.21 | all-reduce | flops 2 | bytes 16 | tf_op jit(solution)/shard_map/pmax | solution.py:183
  (146 shorter events, 56.4 us)
Async XLA Ops:
  7.2 291.0 %copy-start = (bf16[384,1536]{1,0:T(8,128)(2,1)S(1)}, bf16[384,1536]{1,0:T(8,128)(2,1)}, u32[]{:S(2)}) copy-start(bf16[384,1536]{1,0:T(8,128)(2,1)} %param.25) | copy-start | bytes 3538948
  7.2 49.2 %all-gather.10.cloned.1.call-start = ((), (), s32[]{:S(2)}) async-start(), calls=%async_computation.5 | async-start | bytes 3932160 | tf_op jit(solution)/shard_map/all_gather | solution.py:68
  7.9 127.6 %all-gather.8.cloned.1.call-start = ((), (), s32[]{:S(2)}) async-start(), calls=%async_computation.2 | async-start | bytes 3932160 | tf_op jit(solution)/shard_map/all_gather | solution.py:116
  64.3 5.2 copy-start.12
  64.3 14.7 %copy-start.15 = (f32[1,2,2,1536]{3,2,1,0:T(2,128)S(1)}, f32[1,2,2,1536]{3,2,1,0:T(2,128)}, u32[]{:S(2)}) copy-start(f32[1,2,2,1536]{3,2,1,0:T(2,128)} %param.21) | copy-start | bytes 73732
  64.3 135.0 %all-gather.6.cloned.1.call-start = ((), (), s32[]{:S(2)}) async-start(), calls=%async_computation.1 | async-start | bytes 3932160 | tf_op jit(solution)/shard_map/all_gather | solution.py:115
  69.3 48.2 %copy-start.19 = (s32[1,2]{1,0:T(1,128)S(1)}, s32[1,2]{1,0:T(1,128)}, u32[]{:S(2)}) copy-start(s32[1,2]{1,0:T(1,128)} %param.30) | copy-start | bytes 28
  69.4 318.3 %all-reduce.4.cloned.1.call-start = ((), (), s32[]{:S(2)}) async-start(), calls=%async_computation.3 | async-start | bytes 6291456 | tf_op jit(solution)/shard_map/psum | solution.py:139
  214.4 6.9 %copy-start.6 = (f32[2,6,512]{2,1,0:T(8,128)S(1)}, f32[2,6,512]{2,1,0:T(8,128)}, u32[]{:S(2)}) copy-start(f32[2,6,512]{2,1,0:T(8,128)} %get-tuple-element.187) | copy-start | bytes 73732 | tf_op jit(solution)/shard_map/while
  214.4 6.9 %copy-start.8 = (f32[2,6,512]{2,1,0:T(8,128)S(1)}, f32[2,6,512]{2,1,0:T(8,128)}, u32[]{:S(2)}) copy-start(f32[2,6,512]{2,1,0:T(8,128)} %get-tuple-element.188) | copy-start | bytes 73732 | tf_op jit(solution)/shard_map/while
  214.4 8.2 %copy-start.1 = (f32[2,6,512,512]{3,2,1,0:T(8,128)S(1)}, f32[2,6,512,512]{3,2,1,0:T(8,128)}, u32[]{:S(2)}) copy-start(f32[2,6,512,512]{3,2,1,0:T(8,128)} %get-tuple-element.172) | copy-start | bytes 37748740 | tf_op jit(solution)/shard_map/while
  236.3 6.8 %copy-start.6 = (f32[2,6,512]{2,1,0:T(8,128)S(1)}, f32[2,6,512]{2,1,0:T(8,128)}, u32[]{:S(2)}) copy-start(f32[2,6,512]{2,1,0:T(8,128)} %get-tuple-element.187) | copy-start | bytes 73732 | tf_op jit(solution)/shard_map/while
  236.3 6.9 %copy-start.8 = (f32[2,6,512]{2,1,0:T(8,128)S(1)}, f32[2,6,512]{2,1,0:T(8,128)}, u32[]{:S(2)}) copy-start(f32[2,6,512]{2,1,0:T(8,128)} %get-tuple-element.188) | copy-start | bytes 73732 | tf_op jit(solution)/shard_map/while
  236.3 8.2 %copy-start.1 = (f32[2,6,512,512]{3,2,1,0:T(8,128)S(1)}, f32[2,6,512,512]{3,2,1,0:T(8,128)}, u32[]{:S(2)}) copy-start(f32[2,6,512,512]{3,2,1,0:T(8,128)} %get-tuple-element.172) | copy-start | bytes 37748740 | tf_op jit(solution)/shard_map/while
  258.2 6.8 %copy-start.6 = (f32[2,6,512]{2,1,0:T(8,128)S(1)}, f32[2,6,512]{2,1,0:T(8,128)}, u32[]{:S(2)}) copy-start(f32[2,6,512]{2,1,0:T(8,128)} %get-tuple-element.187) | copy-start | bytes 73732 | tf_op jit(solution)/shard_map/while
  258.2 6.9 %copy-start.8 = (f32[2,6,512]{2,1,0:T(8,128)S(1)}, f32[2,6,512]{2,1,0:T(8,128)}, u32[]{:S(2)}) copy-start(f32[2,6,512]{2,1,0:T(8,128)} %get-tuple-element.188) | copy-start | bytes 73732 | tf_op jit(solution)/shard_map/while
  258.2 8.2 %copy-start.1 = (f32[2,6,512,512]{3,2,1,0:T(8,128)S(1)}, f32[2,6,512,512]{3,2,1,0:T(8,128)}, u32[]{:S(2)}) copy-start(f32[2,6,512,512]{3,2,1,0:T(8,128)} %get-tuple-element.172) | copy-start | bytes 37748740 | tf_op jit(solution)/shard_map/while
  280.1 6.8 %copy-start.6 = (f32[2,6,512]{2,1,0:T(8,128)S(1)}, f32[2,6,512]{2,1,0:T(8,128)}, u32[]{:S(2)}) copy-start(f32[2,6,512]{2,1,0:T(8,128)} %get-tuple-element.187) | copy-start | bytes 73732 | tf_op jit(solution)/shard_map/while
  280.1 6.9 %copy-start.8 = (f32[2,6,512]{2,1,0:T(8,128)S(1)}, f32[2,6,512]{2,1,0:T(8,128)}, u32[]{:S(2)}) copy-start(f32[2,6,512]{2,1,0:T(8,128)} %get-tuple-element.188) | copy-start | bytes 73732 | tf_op jit(solution)/shard_map/while
  280.1 8.2 %copy-start.1 = (f32[2,6,512,512]{3,2,1,0:T(8,128)S(1)}, f32[2,6,512,512]{3,2,1,0:T(8,128)}, u32[]{:S(2)}) copy-start(f32[2,6,512,512]{3,2,1,0:T(8,128)} %get-tuple-element.172) | copy-start | bytes 37748740 | tf_op jit(solution)/shard_map/while
  291.6 4.3 copy-start.7
  291.6 4.3 copy-start.10
  291.6 4.3 copy-start.5
  301.7 165.8 %reduce-scatter.4.cloned.1.call-start = ((), (), s32[]{:S(2)}) async-start(), calls=%async_computation.6 | async-start | bytes 3932160
  418.9 5.2 copy-start.16
  423.3 58.2 %copy-start.18 = (bf16[384,64]{0,1:T(8,128)(2,1)S(1)}, bf16[384,64]{0,1:T(8,128)(2,1)}, u32[]{:S(2)}) copy-start(bf16[384,64]{0,1:T(8,128)(2,1)} %param.28) | copy-start | bytes 147460
  423.3 101.5 %all-reduce.6.cloned.1.call-start = ((), (), s32[]{:S(2)}) async-start(), calls=%async_computation.4 | async-start | bytes 262144 | tf_op jit(solution)/shard_map/psum | solution.py:172
  424.1 101.7 %copy-start.20 = (s32[2]{0:T(128)S(1)}, s32[2]{0:T(128)}, u32[]{:S(2)}) copy-start(s32[2]{0:T(128)} %param.31) | copy-start | bytes 28
  424.2 101.7 %copy-start.21 = (s32[2]{0:T(128)S(1)}, s32[2]{0:T(128)}, u32[]{:S(2)}) copy-start(s32[2]{0:T(128)} %param.32) | copy-start | bytes 28
  424.2 103.0 %copy-start.11 = (f32[2,512,32]{1,2,0:T(8,128)S(1)}, f32[2,512,32]{1,2,0:T(8,128)}, u32[]{:S(2)}) copy-start(f32[2,512,32]{1,2,0:T(8,128)} %param.29) | copy-start | bytes 393220
  424.2 102.9 %copy-start.17 = (f32[2]{0:T(128)S(1)}, f32[2]{0:T(128)}, u32[]{:S(2)}) copy-start(f32[2]{0:T(128)} %param.33) | copy-start | bytes 28
  525.8 1.3 collective-permute-start
  (9 other events, 28.5 us)
Sparse Core Ops, SparseCore 0:
  9.8 46.5 all-gather.9
  64.4 71.0 all-gather.7
  137.1 62.2 all-gather.5
  301.8 85.8 all-reduce.3
  423.4 43.9 reduce-scatter.3
  482.9 41.9 all-reduce.5
where the time goes:
time: 553 us; the launch traced here: 552 us
  waiting for transfers between devices  289 us (52%)
  matrix products  85.7 us (15%)
  blocking collectives  68.6 us (12%)
  other arithmetic  47.8 us (9%)
  local copies, waits for them, and re-layouts  45.9 us (8%)
  between operations  14.5 us (3%)
    psum x1, waiting for transfers between devices, per_device(): lax.psum(attn_part.astype(jnp.bfloat16), 'blk').astype(jnp.float32)  85.9 us
    all_gather x1, waiting for transfers between devices, per_device(): key_piece = lax.all_gather(keys_img, 'seq', axis=1, tiled=True)  59.2 us
    all_gather x1, waiting for transfers between devices, per_device(): lax.all_gather(img_hidden[0], 'blk', axis=2, tiled=True)  46.8 us
    unnamed x7, waiting for transfers between devices  44 us
    psum x1, waiting for transfers between devices, per_device(): lax.psum(velocity_part.astype(jnp.bfloat16), 'blk').astype(jnp.float32)  42.1 us
    dot_general x8, matrix products, project(): result = jnp.dot(flat_rows, weight, preferred_element_type=jnp.float32)  37 us
    dot_general x5, matrix products, attend_block(): jnp.einsum('pqhe,pkhe->phqk', query_heads, key_heads, preferred_element_t...  35.9 us
    reduce_sum x5, other arithmetic, attend_block(): denominator = denominator * factor + jnp.sum(weights, axis=-1)  30.6 us
  transfers between devices with their start and end apart: 7, of which 7 were waited for; matrix products, arithmetic and copies ran while one was open for 5% of the time, Pallas kernels for 0%

commit v1 on v0

--- a/solution.py
+++ b/solution.py
@@ -7,6 +7,18 @@
 STEPS = 28
 EPSILON = 1e-06
 BLOCK_ROWS = 512
+
+
+def gather_by_bits(array, axis, dim):
+    ways, here, step = (lax.axis_size(axis), lax.axis_index(axis), array.shape[dim])
+    line, have = (array, 1)
+    while have < ways:
+        line = jnp.concatenate(
+            [line, lax.ppermute(line, axis, [(d, (d - have) % ways) for d in range(ways)])],
+            axis=dim,
+        )
+        have = 2 * have
+    return jnp.roll(line, here * step, axis=dim)
 
 
 def from_partner(value, axis, bit):
@@ -125,7 +137,7 @@
 
     running_state, unused = lax.scan(scan_step, running_state, (key_split, value_split))
     all_text_keys, all_text_values = (
-        lax.all_gather(text_keys, "seq", axis=1, tiled=True),
+        gather_by_bits(text_keys, "seq", 1),
         lax.all_gather(text_values, "seq", axis=1, tiled=True),
     )
     slot_index = jnp.arange(all_text_keys.shape[1], dtype=jnp.int32)

time: 553 us -> 556 us (level)
  blocking collectives: 68.6 us -> 62.6 us
    all_gather x1, waiting for transfers between devices: 59.2 us -> 8.01 us  [per_device(): key_piece = lax.all_gather(keys_img, 'seq', axis=1, tiled=True)]
    all_gather x1, waiting for transfers between devices: 9.59 us -> 59 us  [per_device(): value_piece = lax.all_gather(values_img, 'seq', axis=1, tiled=True)]
    all_gather x1 -> x0, blocking collectives: 16.4 us -> none  [per_device(): lax.all_gather(text_keys, 'seq', axis=1, tiled=True)]
    all_gather x1, blocking collectives: 16.7 us -> 27 us  [per_device(): lax.all_gather(text_values, 'seq', axis=1, tiled=True)]
    unnamed x48 -> x52, local copies, waits for them, and re-layouts: 20.2 us -> 22.8 us
  transfers between devices with their start and end apart: 7 -> 9, of which waited for: 7 -> 8; matrix products, arithmetic and copies ran while one was open for 5% -> 5% of each run, Pallas kernels for 0% -> 0%
where the time goes in v1:
time: 556 us; the launch traced here: 554 us
  waiting for transfers between devices  289 us (52%)
  matrix products  86.4 us (16%)
  blocking collectives  62.6 us (11%)
  local copies, waits for them, and re-layouts  49.2 us (9%)
  other arithmetic  47.8 us (9%)
  between operations  14.5 us (3%)
    psum x1, waiting for transfers between devices, per_device(): lax.psum(attn_part.astype(jnp.bfloat16), 'blk').astype(jnp.float32)  85.9 us
    all_gather x1, waiting for transfers between devices, per_device(): value_piece = lax.all_gather(values_img, 'seq', axis=1, tiled=True)  59 us
    all_gather x1, waiting for transfers between devices, per_device(): lax.all_gather(img_hidden[0], 'blk', axis=2, tiled=True)  46.8 us
    unnamed x7, waiting for transfers between devices  44 us
    psum x1, waiting for transfers between devices, per_device(): lax.psum(velocity_part.astype(jnp.bfloat16), 'blk').astype(jnp.float32)  42.1 us
    dot_general x8, matrix products, project(): result = jnp.dot(flat_rows, weight, preferred_element_type=jnp.float32)  37.7 us
    dot_general x5, matrix products, attend_block(): jnp.einsum('pqhe,pkhe->phqk', query_heads, key_heads, preferred_element_t...  35.8 us
    reduce_sum x5, other arithmetic, attend_block(): denominator = denominator * factor + jnp.sum(weights, axis=-1)  30.6 us
  transfers between devices with their start and end apart: 9, of which 8 were waited for; matrix products, arithmetic and copies ran while one was open for 5% of the time, Pallas kernels for 0%

profile of v1, /device:TPU:0, one launch (start us, length us, event | category | flops | bytes accessed | tf_op | source)
XLA Modules:
  0.0 554.4 jit_solution(5784932743576147067)
XLA Ops:
  9.6 46.8 %all-gather.10.cloned.1.call-done = bf16[1,2,512,1536]{3,2,1,0:T(8,128)(2,1)} async-done(((bf16[1,2,512,384]{3,2,1,0:T(8,128)(2,1)}), bf16[1,2,512,1536]{3,2,1,0:T(8,128)(2,1)}) %all-gather.10.cloned.1.call-update) | async-done | bytes 3145744 | tf_op jit(solution)/shard_map/all_gather | solution.py:80
  60.2 4.0 convolution_convert_fusion.3
  64.4 5.0 convolution_convert_fusion.1
  69.4 9.2 %all-gather.1 = bf16[1,2,40,1536]{3,2,1,0:T(8,128)(2,1)S(1)} all-gather(bf16[1,2,40,384]{3,2,1,0:T(8,128)(2,1)S(1)} %copy-done.12), channel_id=3, replica_groups=mesh['cfg'=2,'seq'=4,'blk'=4] {'blk'}, dimensions={3}, use_global_device_ids=true | all-gather | bytes 307200 | tf_op jit(solution)/shard_map/all_gather | solution.py:81
  81.4 3.3 collective-permute-start
  89.4 27.0 %all_gather.19 = bf16[2,160,384]{2,1,0:T(8,128)(2,1)S(1)} all-gather(bf16[2,40,384]{2,1,0:T(8,128)(2,1)S(1)} %fusion.82), channel_id=1, replica_groups=mesh['cfg'=2,'seq'=4,'blk'=4] {'seq'}, dimensions={1}, use_global_device_ids=true | all-gather | bytes 307200 | tf_op jit(solution)/shard_map/all_gather | solution.py:141
  121.7 4.1 convolution_convert_fusion.2
  126.7 3.4 fusion.41
  130.1 8.0 %all-gather.6.cloned.1.call-done = bf16[2,2048,384]{2,1,0:T(8,128)(2,1)} async-done(((bf16[2,512,384]{2,1,0:T(8,128)(2,1)}), bf16[2,2048,384]{2,1,0:T(8,128)(2,1)}) %all-gather.6.cloned.1.call-update) | async-done | bytes 3145744 | tf_op jit(solution)/shard_map/all_gather | solution.py:127
  138.1 4.7 copy.35
  142.8 59.0 %all-gather.8.cloned.1.call-done = bf16[2,2048,384]{2,1,0:T(8,128)(2,1)} async-done(((bf16[2,512,384]{2,1,0:T(8,128)(2,1)}), bf16[2,2048,384]{2,1,0:T(8,128)(2,1)}) %all-gather.8.cloned.1.call-update) | async-done | bytes 3145744 | tf_op jit(solution)/shard_map/all_gather | solution.py:128
  201.8 4.7 copy.37
  206.5 87.5 %while.15 = (s32[]{:T(128)}, f32[2,6,512,64]{2,3,1,0:T(8,128)S(1)}, f32[2,6,512]{2,1,0:T(8,128)}, f32[2,6,512]{2,1,0:T(8,128)}, bf16[4,2,512,384]{2,3,1,0:T(8,12...) while((s32[]{:T(128)}, f32[2,6,512,64]{2,3,1,0:T(8,128)S(1)}, ...), condition=%wide.region_5.0_spmd.clone, body=%wide.region_2.5_spmd.clone.sunk | while | flops 831682560 | bytes 97419496 | solution.py:138
  208.0 8.1 %bitcast_reduce_fusion.2 = (f32[2,6,512]{2,1,0:T(8,128)}, f32[2,6,512,512]{3,2,1,0:T(8,128)}) fusion(bf16[2,512,6,64]{1,3,2,0:T(8,128)(2,1)S(1)} %bitcast.169, bf16[2,512,6,64]{1,3,2,0:T(8,128)(2,1)} %get-tuple-element.201), kind=kOutput, calls=%fused_computation.1.clone.1 | convolution fusion | flops 408938496 | bytes 14180352 | tf_op jit(solution)/shard_map/while/body/eval_jaxpr/pqhe,pkhe->phqk/dot_general | solution.py:103
  216.9 6.8 %fusion.134 = f32[2,6,512]{2,1,0:T(8,128)S(1)} fusion(f32[2,6,512,512]{3,2,1,0:T(8,128)} %get-tuple-element.174, f32[2,6,512]{2,1,0:T(8,128)S(1)} %select_maximum_fusion.2), kind=kLoop, calls=%fused_computation.3.clone.1 | loop fusion | flops 9431040 | bytes 12632064 | tf_op jit(solution)/shard_map/while/body/eval_jaxpr/reduce_sum | solution.py:111
  229.9 8.1 %bitcast_reduce_fusion.2 = (f32[2,6,512]{2,1,0:T(8,128)}, f32[2,6,512,512]{3,2,1,0:T(8,128)}) fusion(bf16[2,512,6,64]{1,3,2,0:T(8,128)(2,1)S(1)} %bitcast.169, bf16[2,512,6,64]{1,3,2,0:T(8,128)(2,1)} %get-tuple-element.201), kind=kOutput, calls=%fused_computation.1.clone.1 | convolution fusion | flops 408938496 | bytes 14180352 | tf_op jit(solution)/shard_map/while/body/eval_jaxpr/pqhe,pkhe->phqk/dot_general | solution.py:103
  238.8 6.8 %fusion.134 = f32[2,6,512]{2,1,0:T(8,128)S(1)} fusion(f32[2,6,512,512]{3,2,1,0:T(8,128)} %get-tuple-element.174, f32[2,6,512]{2,1,0:T(8,128)S(1)} %select_maximum_fusion.2), kind=kLoop, calls=%fused_computation.3.clone.1 | loop fusion | flops 9431040 | bytes 12632064 | tf_op jit(solution)/shard_map/while/body/eval_jaxpr/reduce_sum | solution.py:111
  251.8 8.1 %bitcast_reduce_fusion.2 = (f32[2,6,512]{2,1,0:T(8,128)}, f32[2,6,512,512]{3,2,1,0:T(8,128)}) fusion(bf16[2,512,6,64]{1,3,2,0:T(8,128)(2,1)S(1)} %bitcast.169, bf16[2,512,6,64]{1,3,2,0:T(8,128)(2,1)} %get-tuple-element.201), kind=kOutput, calls=%fused_computation.1.clone.1 | convolution fusion | flops 408938496 | bytes 14180352 | tf_op jit(solution)/shard_map/while/body/eval_jaxpr/pqhe,pkhe->phqk/dot_general | solution.py:103
  260.7 6.8 %fusion.134 = f32[2,6,512]{2,1,0:T(8,128)S(1)} fusion(f32[2,6,512,512]{3,2,1,0:T(8,128)} %get-tuple-element.174, f32[2,6,512]{2,1,0:T(8,128)S(1)} %select_maximum_fusion.2), kind=kLoop, calls=%fused_computation.3.clone.1 | loop fusion | flops 9431040 | bytes 12632064 | tf_op jit(solution)/shard_map/while/body/eval_jaxpr/reduce_sum | solution.py:111
  273.6 8.1 %bitcast_reduce_fusion.2 = (f32[2,6,512]{2,1,0:T(8,128)}, f32[2,6,512,512]{3,2,1,0:T(8,128)}) fusion(bf16[2,512,6,64]{1,3,2,0:T(8,128)(2,1)S(1)} %bitcast.169, bf16[2,512,6,64]{1,3,2,0:T(8,128)(2,1)} %get-tuple-element.201), kind=kOutput, calls=%fused_computation.1.clone.1 | convolution fusion | flops 408938496 | bytes 14180352 | tf_op jit(solution)/shard_map/while/body/eval_jaxpr/pqhe,pkhe->phqk/dot_general | solution.py:103
  282.6 6.8 %fusion.134 = f32[2,6,512]{2,1,0:T(8,128)S(1)} fusion(f32[2,6,512,512]{3,2,1,0:T(8,128)} %get-tuple-element.174, f32[2,6,512]{2,1,0:T(8,128)S(1)} %select_maximum_fusion.2), kind=kLoop, calls=%fused_computation.3.clone.1 | loop fusion | flops 9431040 | bytes 12632064 | tf_op jit(solution)/shard_map/while/body/eval_jaxpr/reduce_sum | solution.py:111
  295.0 3.4 fusion.47
  300.6 3.5 convolution_convert_fusion
  304.2 85.9 %all-reduce.4.cloned.1.call-done = bf16[2,512,1536]{2,1,0:T(8,128)(2,1)} async-done(((bf16[2,512,1536]{2,1,0:T(8,128)(2,1)}), bf16[2,512,1536]{2,1,0:T(8,128)(2,1)}) %all-reduce.4.cloned.1.call-update) | async-done | bytes 3145744 | tf_op jit(solution)/shard_map/psum | solution.py:151
  390.2 4.0 convert_reduce_fusion.1
  396.8 15.9 %fusion.38 = bf16[2,512,1536]{2,1,0:T(8,128)(2,1)} fusion(bf16[1536,1536]{1,0:T(8,128)(2,1)} %param.27, bf16[1536,1536]{1,0:T(8,128)(2,1)} %param.26, bf16[2,512,1536]{2,1,0:T(8,128)(2,1)} %copy-done.4, f32[2,1536]{1,0:T(2,128)S(1)} %get-tuple-element.115, f32[2,1536]{1,0:T(2,128)S(1)} %get-tuple-element.116, f32[2,512]{1,0:T(2,128)S(1)} %add_rsqrt_fusion.1, ...), kind=kOutput, calls=%fused_computation.50 | convolution fusion | flops 9688842240 | bytes 15761408 | tf_op jit(solution)/shard_map/dot_general | solution.py:43
  412.7 8.6 %copy.43 = bf16[2,512,1536]{1,0,2:T(2,128)(2,1)} copy(bf16[2,512,1536]{2,1,0:T(8,128)(2,1)} %fusion.38) | data formatting | bytes 6291456
  421.4 4.4 copy.56
  426.7 43.2 %reduce-scatter.4.cloned.1.call-done = bf16[384,1024]{1,0:T(8,128)(2,1)} async-done(((bf16[1536,1024]{1,0:T(8,128)(2,1)}), bf16[384,1024]{1,0:T(8,128)(2,1)}) %reduce-scatter.4.cloned.1.call-update) | async-done | bytes 786448
  474.9 9.1 %all-reduce = (f32[2,512]{1,0:T(2,128)S(1)}, f32[2,512]{1,0:T(2,128)S(1)}) all-reduce(f32[2,512]{1,0:T(2,128)S(1)} %get-tuple-element.69, f32[2,512]{1,0:T(2,128)S(1)} %get-tuple-element.68), channel_id=1, replica_groups=mesh['cfg'=2,'seq'=4,'blk'=4] {'blk'}, use_global_device_ids=true, to_apply=%region_17.18 | all-reduce | flops 2048 | bytes 16384 | tf_op jit(solution)/shard_map/psum | solution.py:166
  485.2 42.1 %all-reduce.6.cloned.1.call-done = bf16[2,512,64]{1,2,0:T(8,128)(2,1)} async-done(((bf16[2,512,64]{1,2,0:T(8,128)(2,1)}), bf16[2,512,64]{1,2,0:T(8,128)(2,1)}) %all-reduce.6.cloned.1.call-update) | async-done | bytes 131088 | tf_op jit(solution)/shard_map/psum | solution.py:184
  530.4 17.2 %pmax.7 = f32[2]{0:T(128)} all-reduce(f32[2]{0:T(128)S(1)} %get-tuple-element.97), channel_id=1, replica_groups=mesh['cfg'=2,'seq'=4,'blk'=4] {'cfg','seq'}, use_global_device_ids=true, to_apply=%region_20.21 | all-reduce | flops 2 | bytes 16 | tf_op jit(solution)/shard_map/pmax | solution.py:195
  (156 shorter events, 63.1 us)
Async XLA Ops:
  7.2 293.4 %copy-start = (bf16[384,1536]{1,0:T(8,128)(2,1)S(1)}, bf16[384,1536]{1,0:T(8,128)(2,1)}, u32[]{:S(2)}) copy-start(bf16[384,1536]{1,0:T(8,128)(2,1)} %param.25) | copy-start | bytes 3538948
  7.2 49.2 %all-gather.10.cloned.1.call-start = ((), (), s32[]{:S(2)}) async-start(), calls=%async_computation.5 | async-start | bytes 3932160 | tf_op jit(solution)/shard_map/all_gather | solution.py:80
  7.9 130.2 %all-gather.6.cloned.1.call-start = ((), (), s32[]{:S(2)}) async-start(), calls=%async_computation.1 | async-start | bytes 3932160 | tf_op jit(solution)/shard_map/all_gather | solution.py:127
  64.3 5.1 copy-start.12
  64.3 14.7 %copy-start.15 = (f32[1,2,2,1536]{3,2,1,0:T(2,128)S(1)}, f32[1,2,2,1536]{3,2,1,0:T(2,128)}, u32[]{:S(2)}) copy-start(f32[1,2,2,1536]{3,2,1,0:T(2,128)} %param.21) | copy-start | bytes 73732
  64.3 137.5 %all-gather.8.cloned.1.call-start = ((), (), s32[]{:S(2)}) async-start(), calls=%async_computation.2 | async-start | bytes 3932160 | tf_op jit(solution)/shard_map/all_gather | solution.py:128
  69.3 17.1 %copy-start.19 = (s32[1,2]{1,0:T(1,128)S(1)}, s32[1,2]{1,0:T(1,128)}, u32[]{:S(2)}) copy-start(s32[1,2]{1,0:T(1,128)} %param.30) | copy-start | bytes 28
  69.4 320.8 %all-reduce.4.cloned.1.call-start = ((), (), s32[]{:S(2)}) async-start(), calls=%async_computation.3 | async-start | bytes 6291456 | tf_op jit(solution)/shard_map/psum | solution.py:151
  81.4 6.9 %collective-permute-start = (bf16[2,40,384]{2,1,0:T(8,128)(2,1)S(1)}, bf16[2,40,384]{2,1,0:T(8,128)(2,1)S(1)}, u32[]{:S(2)}, u32[]{:S(2)}) collective-permute-start(bf16[2,40,384]{2,1,0:T(8,128)(2,1)S(1)} %get-tuple-element.112), channel_id=1, source_target_pairs={{0,12},{4,0},{8,4},{12,8},{1,13},{5,1},{9,5},{13,9},{2,14},{6,2},{... | collective-permute-start | bytes 184328 | tf_op jit(solution)/shard_map/ppermute | solution.py:17
  88.2 29.7 %collective-permute-start.1 = (bf16[2,80,384]{2,1,0:T(8,128)(2,1)S(1)}, bf16[2,80,384]{2,1,0:T(8,128)(2,1)S(1)}, u32[]{:S(2)}, u32[]{:S(2)}) collective-permute-start(bf16[2,80,384]{2,1,0:T(8,128)(2,1)S(1)} %pad_maximum_fusion), channel_id=1, source_target_pairs={{0,8},{4,12},{8,0},{12,4},{1,9},{5,13},{9,1},{13,5},{2,10},{6,14},... | collective-permute-start | bytes 368648 | tf_op jit(solution)/shard_map/ppermute | solution.py:17
  216.9 6.9 %copy-start.6 = (f32[2,6,512]{2,1,0:T(8,128)S(1)}, f32[2,6,512]{2,1,0:T(8,128)}, u32[]{:S(2)}) copy-start(f32[2,6,512]{2,1,0:T(8,128)} %get-tuple-element.189) | copy-start | bytes 73732 | tf_op jit(solution)/shard_map/while
  216.9 6.9 %copy-start.8 = (f32[2,6,512]{2,1,0:T(8,128)S(1)}, f32[2,6,512]{2,1,0:T(8,128)}, u32[]{:S(2)}) copy-start(f32[2,6,512]{2,1,0:T(8,128)} %get-tuple-element.190) | copy-start | bytes 73732 | tf_op jit(solution)/shard_map/while
  216.9 8.2 %copy-start.1 = (f32[2,6,512,512]{3,2,1,0:T(8,128)S(1)}, f32[2,6,512,512]{3,2,1,0:T(8,128)}, u32[]{:S(2)}) copy-start(f32[2,6,512,512]{3,2,1,0:T(8,128)} %get-tuple-element.174) | copy-start | bytes 37748740 | tf_op jit(solution)/shard_map/while
  238.8 6.8 %copy-start.6 = (f32[2,6,512]{2,1,0:T(8,128)S(1)}, f32[2,6,512]{2,1,0:T(8,128)}, u32[]{:S(2)}) copy-start(f32[2,6,512]{2,1,0:T(8,128)} %get-tuple-element.189) | copy-start | bytes 73732 | tf_op jit(solution)/shard_map/while
  238.8 6.9 %copy-start.8 = (f32[2,6,512]{2,1,0:T(8,128)S(1)}, f32[2,6,512]{2,1,0:T(8,128)}, u32[]{:S(2)}) copy-start(f32[2,6,512]{2,1,0:T(8,128)} %get-tuple-element.190) | copy-start | bytes 73732 | tf_op jit(solution)/shard_map/while
  238.8 8.2 %copy-start.1 = (f32[2,6,512,512]{3,2,1,0:T(8,128)S(1)}, f32[2,6,512,512]{3,2,1,0:T(8,128)}, u32[]{:S(2)}) copy-start(f32[2,6,512,512]{3,2,1,0:T(8,128)} %get-tuple-element.174) | copy-start | bytes 37748740 | tf_op jit(solution)/shard_map/while
  260.7 6.8 %copy-start.6 = (f32[2,6,512]{2,1,0:T(8,128)S(1)}, f32[2,6,512]{2,1,0:T(8,128)}, u32[]{:S(2)}) copy-start(f32[2,6,512]{2,1,0:T(8,128)} %get-tuple-element.189) | copy-start | bytes 73732 | tf_op jit(solution)/shard_map/while
  260.7 6.9 %copy-start.8 = (f32[2,6,512]{2,1,0:T(8,128)S(1)}, f32[2,6,512]{2,1,0:T(8,128)}, u32[]{:S(2)}) copy-start(f32[2,6,512]{2,1,0:T(8,128)} %get-tuple-element.190) | copy-start | bytes 73732 | tf_op jit(solution)/shard_map/while
  260.7 8.2 %copy-start.1 = (f32[2,6,512,512]{3,2,1,0:T(8,128)S(1)}, f32[2,6,512,512]{3,2,1,0:T(8,128)}, u32[]{:S(2)}) copy-start(f32[2,6,512,512]{3,2,1,0:T(8,128)} %get-tuple-element.174) | copy-start | bytes 37748740 | tf_op jit(solution)/shard_map/while
  282.5 6.8 %copy-start.6 = (f32[2,6,512]{2,1,0:T(8,128)S(1)}, f32[2,6,512]{2,1,0:T(8,128)}, u32[]{:S(2)}) copy-start(f32[2,6,512]{2,1,0:T(8,128)} %get-tuple-element.189) | copy-start | bytes 73732 | tf_op jit(solution)/shard_map/while
  282.5 6.9 %copy-start.8 = (f32[2,6,512]{2,1,0:T(8,128)S(1)}, f32[2,6,512]{2,1,0:T(8,128)}, u32[]{:S(2)}) copy-start(f32[2,6,512]{2,1,0:T(8,128)} %get-tuple-element.190) | copy-start | bytes 73732 | tf_op jit(solution)/shard_map/while
  282.5 8.2 %copy-start.1 = (f32[2,6,512,512]{3,2,1,0:T(8,128)S(1)}, f32[2,6,512,512]{3,2,1,0:T(8,128)}, u32[]{:S(2)}) copy-start(f32[2,6,512,512]{3,2,1,0:T(8,128)} %get-tuple-element.174) | copy-start | bytes 37748740 | tf_op jit(solution)/shard_map/while
  294.0 4.3 copy-start.5
  304.1 165.8 %reduce-scatter.4.cloned.1.call-start = ((), (), s32[]{:S(2)}) async-start(), calls=%async_computation.6 | async-start | bytes 3932160
  421.3 5.2 copy-start.16
  425.8 58.2 %copy-start.18 = (bf16[384,64]{0,1:T(8,128)(2,1)S(1)}, bf16[384,64]{0,1:T(8,128)(2,1)}, u32[]{:S(2)}) copy-start(bf16[384,64]{0,1:T(8,128)(2,1)} %param.28) | copy-start | bytes 147460
  425.8 101.5 %all-reduce.6.cloned.1.call-start = ((), (), s32[]{:S(2)}) async-start(), calls=%async_computation.4 | async-start | bytes 262144 | tf_op jit(solution)/shard_map/psum | solution.py:184
  426.6 101.7 %copy-start.20 = (s32[2]{0:T(128)S(1)}, s32[2]{0:T(128)}, u32[]{:S(2)}) copy-start(s32[2]{0:T(128)} %param.31) | copy-start | bytes 28
  426.6 101.7 %copy-start.21 = (s32[2]{0:T(128)S(1)}, s32[2]{0:T(128)}, u32[]{:S(2)}) copy-start(s32[2]{0:T(128)} %param.32) | copy-start | bytes 28
  426.7 102.9 %copy-start.11 = (f32[2,512,32]{1,2,0:T(8,128)S(1)}, f32[2,512,32]{1,2,0:T(8,128)}, u32[]{:S(2)}) copy-start(f32[2,512,32]{1,2,0:T(8,128)} %param.29) | copy-start | bytes 393220
  426.7 102.9 %copy-start.17 = (f32[2]{0:T(128)S(1)}, f32[2]{0:T(128)}, u32[]{:S(2)}) copy-start(f32[2]{0:T(128)} %param.33) | copy-start | bytes 28
  528.3 1.3 collective-permute-start.2
  (11 other events, 37.2 us)
Sparse Core Ops, SparseCore 0:
  9.8 46.5 all-gather.9
  64.4 73.6 all-gather.5
  139.7 62.1 all-gather.7
  304.3 85.8 all-reduce.3
  425.9 43.9 reduce-scatter.3
  485.3 41.9 all-reduce.5
